TPU v7x, 32 devices: a whole 2x2x4 slice. The times are simulated.
32 devices in a mesh: grp: 2 (over x), pool: 16 (over z, y, core).
Axes of the slice: x: 2, y: 2, z: 4, core: 2. Of those that a mesh axis runs over, the one named last changes fastest.
Arguments:
- queries: bfloat16 [32, 128, 1024], P(('grp', 'pool')), parts along dimension 0, may hold values from -400 to 400
- new_kv: bfloat16 [32, 128, 256], P(('grp', 'pool')), parts along dimension 0, may hold values from -16 to 16
- pool_kv: bfloat16 [64, 8, 128, 256], P(('grp', 'pool')), parts along dimension 0, may hold values from -16 to 16
- hit_slots: int32 [4, 16], P('grp'), parts along dimension 0, may hold values from 0 to 31, as said below
- prefix_blocks: int32 [4], P('grp'), parts along dimension 0, may hold values from 1 to 16, 20 in all
- new_owners: int32 [4, 2], P('grp'), parts along dimension 0, may hold values from 0 to 15, as said below
Outputs:
- attended: bfloat16 [32, 128, 1024], P(('grp', 'pool')), parts along dimension 0
- new_store: bfloat16 [32, 8, 128, 256], P(('grp', 'pool')), parts along dimension 0
There are 2 independent parts, one for each index of `grp`. A program takes and returns all parts, laid end to end along the dimension named above; each array names one. Nothing has to cross between parts.
Inputs may be any that keep to these rules, and one draw needn't show every extreme that they name: `hit_slots`: slot s lies on owner s // 2. Block j of request r lies on owner (f + j) mod 16, where f depends on r and is a multiple of 4; one owner keeps different requests in different slots. Entries with j >= prefix_blocks[r] are unused. `prefix_blocks`: they sum to 20. `new_owners`: all 4 entries are distinct.
All inputs are finite; a program needn't handle non-finite values.
Results may differ from a plain program's by a relative error of at most 0.009.
Values may be sent and summed in bfloat16 or wider, within the bound.
A program may use at most 64 MiB of HBM per device.

v0:
```python
import math

import jax
import jax.numpy as jnp
from jax import lax
from jax.sharding import PartitionSpec as P

group_slots = 4
minus_big = -1e30


def fold_keys(state_now, query_rows, key_rows, values, usable, score_scale):
    maximum, totals, accumulated = state_now
    scores = (
        jnp.einsum("tgd,kd->tgk", query_rows, key_rows, preferred_element_type=jnp.float32)
        * score_scale
    )
    scores = jnp.where(usable, scores, minus_big)
    maximum_new = jnp.maximum(maximum, jnp.max(scores, axis=2))
    weights = jnp.where(usable, jnp.exp(scores - maximum_new[:, :, None]), 0.0)
    factor = jnp.exp(maximum - maximum_new)
    totals = totals * factor + jnp.sum(weights, axis=2)
    accumulated = accumulated * factor[:, :, None] + jnp.einsum(
        "tgk,kd->tgd", weights.astype(jnp.bfloat16), values, preferred_element_type=jnp.float32
    )
    return (maximum_new, totals, accumulated)


def attend_blocks(state_now, query_rows, stored, first_slot, live_count, score_scale):
    slot_total = stored.shape[0]
    block_len = stored.shape[1]
    row_width = stored.shape[2]
    head_dim = row_width // 2
    loop_steps = (live_count + group_slots - 1) // group_slots
    offsets = jnp.arange(group_slots * block_len, dtype=jnp.int32) // block_len

    def advance(turn_index, state_in):
        start_slot = (first_slot + turn_index * group_slots) % slot_total
        block_rows = lax.dynamic_slice_in_dim(stored, start_slot, group_slots, 0).reshape(
            group_slots * block_len, row_width
        )
        usable = (turn_index * group_slots + offsets < live_count)[None, None, :]
        return fold_keys(
            state_in,
            query_rows,
            block_rows[:, :head_dim],
            block_rows[:, head_dim:],
            usable,
            score_scale,
        )

    return lax.fori_loop(0, loop_steps, advance, state_now)


def on_device(queries, new_kv, pool_kv, hit_slots, prefix_blocks, new_owners):
    my_index = lax.axis_index("pool")
    slot_count = pool_kv.shape[0]
    kv_heads = pool_kv.shape[1]
    block_len = pool_kv.shape[2]
    row_width = pool_kv.shape[3]
    head_dim = row_width // 2
    requests = hit_slots.shape[0]
    longest = hit_slots.shape[1]
    groups = queries.shape[2] // head_dim
    score_scale = 1.0 / math.sqrt(head_dim)
    request = my_index // kv_heads
    positions = jnp.arange(longest, dtype=jnp.int32)
    is_live = positions[None, :] < prefix_blocks[:, None]
    on_me = (hit_slots // slot_count == my_index) & is_live
    holds_block = jnp.any(on_me, axis=1)
    local_slot = jnp.sum(jnp.where(on_me, hit_slots % slot_count, 0), axis=1)
    picked = jnp.take(pool_kv, local_slot, axis=0)
    outgoing = jnp.where(holds_block[:, None, None, None], picked, jnp.zeros_like(picked))
    outgoing = outgoing.reshape(requests * kv_heads, block_len, row_width)
    fetched = lax.all_to_all(outgoing, "pool", split_axis=0, concat_axis=0, tiled=True)
    query_rows = queries[0].reshape(block_len, groups, head_dim)
    own_new = new_kv[0]
    causal = (jnp.arange(block_len)[None, :] <= jnp.arange(block_len)[:, None])[:, None, :]
    empty_state = (
        jnp.full((block_len, groups), minus_big, jnp.float32),
        jnp.zeros((block_len, groups), jnp.float32),
        jnp.zeros((block_len, groups, head_dim), jnp.float32),
    )
    state_now = fold_keys(
        empty_state, query_rows, own_new[:, :head_dim], own_new[:, head_dim:], causal, score_scale
    )
    own_length = prefix_blocks[request]
    own_first = hit_slots[request, 0] // slot_count
    state_now = attend_blocks(state_now, query_rows, fetched, own_first, own_length, score_scale)
    attended = (
        (state_now[2] / state_now[1][:, :, None])
        .reshape(block_len, groups * head_dim)
        .astype(jnp.bfloat16)[None]
    )
    arrived = lax.all_gather(new_kv, "pool", axis=0, tiled=True)
    owned_by_me = jnp.any(new_owners == my_index, axis=1)
    source_request = jnp.sum(jnp.where(owned_by_me, jnp.arange(requests, dtype=jnp.int32), 0))
    owned = jnp.any(owned_by_me)
    new_block = lax.dynamic_slice_in_dim(arrived, source_request * kv_heads, kv_heads, 0)
    new_store = jnp.where(owned, new_block, jnp.zeros_like(new_block))[None]
    return (attended, new_store)


def solution(mesh):
    placed = (
        P(("grp", "pool"), None, None),
        P(("grp", "pool"), None, None),
        P(("grp", "pool"), None, None, None),
        P("grp", None),
        P("grp"),
        P("grp", None),
    )
    return jax.shard_map(
        on_device,
        mesh=mesh,
        in_specs=placed,
        out_specs=(P(("grp", "pool"), None, None), P(("grp", "pool"), None, None, None)),
        check_vma=False,
    )
```

profile of v0, /device:TPU:0, one launch (start us, length us, event | category | flops | bytes accessed | tf_op | source)
XLA Modules:
  0.0 75.0 jit_solution(3903400085508740048)
XLA Ops:
  7.2 0.0 copy-start
  7.2 1.0 %fusion.36 = (pred[2]{0:T(512)(128)(4,1)S(1)}, pred[2,16]{1,0:T(4,128)(4,1)S(1)}) fusion(s32[2]{0:T(128)} %param.12, s32[]{:T(128)S(6)} %axis_index.12, s32[2,16]{1,0:T(2,128)} %param.11), kind=kLoop, calls=%fused_computation.73 | loop fusion | flops 606 | bytes 174 | tf_op jit(solution)/shard_map/reduce_or | solution.py:70
  8.2 0.8 %fusion.30 = s32[2]{0:T(128)S(1)} fusion(pred[2,16]{1,0:T(4,128)(4,1)S(1)} %get-tuple-element.196, s32[2,16]{1,0:T(2,128)} %param.11), kind=kLoop, calls=%fused_computation.62 | loop fusion | flops 414 | bytes 168 | tf_op jit(solution)/shard_map/reduce_sum | solution.py:71
  9.0 0.1 broadcast_in_dim.117
  9.1 0.1 broadcast_in_dim.118
  9.1 0.1 broadcast_in_dim.114
  9.2 0.1 broadcast_in_dim.115
  9.3 0.0 copy-done
  9.3 0.6 gather_fusion
  9.9 0.0 copy-start.3
  9.9 0.0 copy-start.5
  10.0 0.0 copy-start.2
  10.0 1.3 %fusion.22 = bf16[16,128,256]{2,1,0:T(8,128)(2,1)} fusion(bf16[2,8,128,256]{3,2,1,0:T(8,128)(2,1)S(1)} %gather_fusion, pred[16]{0:T(512)(128)(4,1)S(1)} %broadcast_in_dim.118, pred[16]{0:T(512)(128)(4,1)S(1)} %broadcast_in_dim.115), kind=kLoop, calls=%fused_computation.37 | loop fusion | flops 1048576 | bytes 2097184 | tf_op jit(solution)/shard_map/jit(_where)/select_n | solution.py:73
  11.3 0.0 copy-start.4
  11.3 0.0 copy-start.1
  11.3 7.5 %all-to-all-start = ((bf16[16,128,256]{2,1,0:T(8,128)(2,1)}), bf16[16,128,256]{2,1,0:T(8,128)(2,1)S(1)}, u32[]{:S(2)}, u32[]{:S(2)}) async-start(bf16[16,128,256]{2,1,0:T(8,128)(2,1)} %fusion.22), calls=%async_computation | async-start | bytes 2097152 | tf_op jit(solution)/shard_map/all_to_all | solution.py:75
  18.8 0.0 all-gather.2.cloned.1.call-start
  18.8 0.7 all-gather.2.cloned.1.call-update
  19.5 0.0 copy-done.3
  19.6 0.5 constant_dynamic-slice_fusion.1
  22.7 0.0 copy-done.5
  22.7 0.6 dynamic_slice.15
  24.0 0.0 copy-done.2
  24.0 0.2 copy.18
  24.1 0.2 copy.21
  24.3 0.0 copy-done.4
  24.3 0.7 fusion.34
  25.0 0.7 select_reduce_fusion
  26.3 0.0 copy-done.1
  26.3 0.2 fusion.37
  26.6 0.1 fusion.24
  26.7 0.3 convolution_add_fusion.1
  27.0 15.8 %all-to-all-done = bf16[16,128,256]{2,1,0:T(8,128)(2,1)S(1)} async-done(((bf16[16,128,256]{2,1,0:T(8,128)(2,1)}), bf16[16,128,256]{2,1,0:T(8,128)(2,1)S(1)}, u32[]{:S(2)}, u32[]{:S(2)}) %all-to-all-start) | async-done | bytes 1048608 | tf_op jit(solution)/shard_map/all_to_all | solution.py:75
  42.9 11.4 %while.17 = (s32[]{:T(128)}, f32[128,8]{0,1:T(8,128)S(1)}, f32[128,8]{0,1:T(8,128)S(1)}, f32[128,8,128]{2,0,1:T(8,128)S(1)}, s32[]{:T(128)}, /*index=5*/s32[]{:T...) while((s32[]{:T(128)}, f32[128,8]{0,1:T(8,128)S(1)}, ...), condition=%wide.region_7.8_spmd.clone, body=%wide.region_4.7_spmd.clone.sunk | while | flops 275520512 | bytes 8457016 | solution.py:52
  42.9 0.7 fusion.46
  43.5 0.5 bitcast_reduce_fusion.2
  44.0 0.6 fusion.47
  44.7 1.0 %convolution_add_fusion.3 = f32[128,8,128]{2,0,1:T(8,128)S(1)} fusion(f32[512,128,8]{1,0,2:T(8,128)S(1)} %get-tuple-element.264, f32[128,8]{0,1:T(8,128)S(1)} %max.8, pred[512]{0:T(512)(128)(4,1)S(1)} %fusion.46, f32[128,8,128]{2,0,1:T(8,128)S(1)} %get-tuple-element.284, f32[128,8]{0,1:T(8,128)S(1)} %get-tuple-element.266, ...), kind=kOutput, calls=%fused_computation.9.clone.1 | convolution fusion | flops 137101312 | bytes 3286016 | tf_op jit(solution)/shard_map/while/body/tgk,kd->tgd/dot_general | solution.py:23
  45.7 0.7 fusion.46
  46.4 0.5 bitcast_reduce_fusion.2
  46.9 0.6 fusion.47
  47.5 1.0 %convolution_add_fusion.3 = f32[128,8,128]{2,0,1:T(8,128)S(1)} fusion(f32[512,128,8]{1,0,2:T(8,128)S(1)} %get-tuple-element.264, f32[128,8]{0,1:T(8,128)S(1)} %max.8, pred[512]{0:T(512)(128)(4,1)S(1)} %fusion.46, f32[128,8,128]{2,0,1:T(8,128)S(1)} %get-tuple-element.284, f32[128,8]{0,1:T(8,128)S(1)} %get-tuple-element.266, ...), kind=kOutput, calls=%fused_computation.9.clone.1 | convolution fusion | flops 137101312 | bytes 3286016 | tf_op jit(solution)/shard_map/while/body/tgk,kd->tgd/dot_general | solution.py:23
  48.6 0.7 fusion.46
  49.3 0.5 bitcast_reduce_fusion.2
  49.8 0.6 fusion.47
  50.4 1.0 %convolution_add_fusion.3 = f32[128,8,128]{2,0,1:T(8,128)S(1)} fusion(f32[512,128,8]{1,0,2:T(8,128)S(1)} %get-tuple-element.264, f32[128,8]{0,1:T(8,128)S(1)} %max.8, pred[512]{0:T(512)(128)(4,1)S(1)} %fusion.46, f32[128,8,128]{2,0,1:T(8,128)S(1)} %get-tuple-element.284, f32[128,8]{0,1:T(8,128)S(1)} %get-tuple-element.266, ...), kind=kOutput, calls=%fused_computation.9.clone.1 | convolution fusion | flops 137101312 | bytes 3286016 | tf_op jit(solution)/shard_map/while/body/tgk,kd->tgd/dot_general | solution.py:23
  51.5 0.7 fusion.46
  52.1 0.5 bitcast_reduce_fusion.2
  52.6 0.6 fusion.47
  53.2 1.0 %convolution_add_fusion.3 = f32[128,8,128]{2,0,1:T(8,128)S(1)} fusion(f32[512,128,8]{1,0,2:T(8,128)S(1)} %get-tuple-element.264, f32[128,8]{0,1:T(8,128)S(1)} %max.8, pred[512]{0:T(512)(128)(4,1)S(1)} %fusion.46, f32[128,8,128]{2,0,1:T(8,128)S(1)} %get-tuple-element.284, f32[128,8]{0,1:T(8,128)S(1)} %get-tuple-element.266, ...), kind=kOutput, calls=%fused_computation.9.clone.1 | convolution fusion | flops 137101312 | bytes 3286016 | tf_op jit(solution)/shard_map/while/body/tgk,kd->tgd/dot_general | solution.py:23
  54.3 0.2 divide_convert_fusion
  54.5 0.2 copy.22
  54.7 0.8 %convert_element_type.24 = bf16[1,128,1024]{2,1,0:T(8,128)(2,1)} reshape(bf16[128,8,128]{2,1,0:T(8,128)(2,1)S(1)} %copy.22) | data formatting | bytes 524288 | tf_op jit(solution)/shard_map/convert_element_type | solution.py:93
  55.5 10.2 %all-gather.2.cloned.1.call-done = bf16[16,128,256]{2,1,0:T(8,128)(2,1)} async-done(((bf16[1,128,256]{2,1,0:T(8,128)(2,1)}), bf16[16,128,256]{2,1,0:T(8,128)(2,1)}) %all-gather.2.cloned.1.call-update) | async-done | bytes 1048592 | tf_op jit(solution)/shard_map/all_gather | solution.py:95
  65.7 2.5 %select_bitcast_fusion = bf16[1,8,128,256]{3,2,1,0:T(8,128)(2,1)} fusion(bf16[16,128,256]{2,1,0:T(8,128)(2,1)} %all-gather.2.cloned.1.call-done, s32[]{:T(128)S(6)} %select_n.133, pred[]{:T(512)} %get-tuple-element.173), kind=kLoop, calls=%fused_computation.38 | loop fusion | flops 262144 | bytes 1048581 | tf_op jit(solution)/shard_map/broadcast_in_dim | solution.py:100
  (22 shorter events, 0.2 us)
Async XLA Ops:
  7.2 2.1 %copy-start = (bf16[2,8,128,256]{3,2,1,0:T(8,128)(2,1)S(1)}, bf16[2,8,128,256]{3,2,1,0:T(8,128)(2,1)}, u32[]{:S(2)}) copy-start(bf16[2,8,128,256]{3,2,1,0:T(8,128)(2,1)} %param.10) | copy-start | bytes 3145732
  9.9 9.6 %copy-start.3 = (s32[2,16]{1,0:T(2,128)S(1)}, s32[2,16]{1,0:T(2,128)}, u32[]{:S(2)}) copy-start(s32[2,16]{1,0:T(2,128)} %param.11) | copy-start | bytes 388
  9.9 12.7 %copy-start.5 = (s32[2]{0:T(128)S(1)}, s32[2]{0:T(128)}, u32[]{:S(2)}) copy-start(s32[2]{0:T(128)} %param.12) | copy-start | bytes 28
  10.0 14.0 %copy-start.2 = (bf16[1,128,1024]{2,1,0:T(8,128)(2,1)S(1)}, bf16[1,128,1024]{2,1,0:T(8,128)(2,1)}, u32[]{:S(2)}) copy-start(bf16[1,128,1024]{2,1,0:T(8,128)(2,1)} %param.8) | copy-start | bytes 786436
  11.3 13.1 %copy-start.4 = (s32[2,2]{1,0:T(2,128)S(1)}, s32[2,2]{1,0:T(2,128)}, u32[]{:S(2)}) copy-start(s32[2,2]{1,0:T(2,128)} %param.13) | copy-start | bytes 52
  11.3 15.1 %copy-start.1 = (bf16[1,128,256]{2,1,0:T(8,128)(2,1)S(1)}, bf16[1,128,256]{2,1,0:T(8,128)(2,1)}, u32[]{:S(2)}) copy-start(bf16[1,128,256]{2,1,0:T(8,128)(2,1)} %param.9) | copy-start | bytes 196612
  11.3 31.6 %all-to-all-start = ((bf16[16,128,256]{2,1,0:T(8,128)(2,1)}), bf16[16,128,256]{2,1,0:T(8,128)(2,1)S(1)}, u32[]{:S(2)}, u32[]{:S(2)}) async-start(bf16[16,128,256]{2,1,0:T(8,128)(2,1)} %fusion.22), calls=%async_computation | async-start | bytes 2097152 | tf_op jit(solution)/shard_map/all_to_all | solution.py:75
  18.8 46.9 %all-gather.2.cloned.1.call-start = ((), (), s32[]{:S(2)}) async-start(), calls=%async_computation.1 | async-start | bytes 1114112 | tf_op jit(solution)/shard_map/all_gather | solution.py:95
Sparse Core Ops, SparseCore 0:
  21.8 43.8 all-gather.1
where the time goes:
time: 75.4 us; the launch traced here: 75 us
  waiting for transfers between devices  26.7 us (35%)
  between operations  18.1 us (24%)
  other arithmetic  12.3 us (16%)
  starting transfers between devices  7.56 us (10%)
  matrix products  6.42 us (9%)
  local copies, waits for them, and re-layouts  3.52 us (5%)
    all_to_all x1, waiting for transfers between devices, on_device(): lax.all_to_all(outgoing, 'pool', split_axis=0, concat_axis=0, tiled=True)  15.8 us
    all_gather x1, waiting for transfers between devices, on_device(): arrived = lax.all_gather(new_kv, 'pool', axis=0, tiled=True)  10.2 us
    all_to_all x1, starting transfers between devices, on_device(): lax.all_to_all(outgoing, 'pool', split_axis=0, concat_axis=0, tiled=True)  7.52 us
    dot_general x5, matrix products, fold_keys(): jnp.einsum('tgk,kd->tgd', weights.astype(jnp.bfloat16), values, preferred...  4.33 us
    lt x4, other arithmetic, advance(): usable = (turn_index * group_slots + offsets < live_count)[None, None, :]  2.62 us
    reduce_sum x5, other arithmetic, fold_keys(): totals = totals * factor + jnp.sum(weights, axis=2)  2.53 us
    broadcast_in_dim x1, other arithmetic, on_device(): new_store = jnp.where(owned, new_block, jnp.zeros_like(new_block))[None]  2.49 us
    dot_general x5, matrix products, fold_keys(): jnp.einsum('tgd,kd->tgk', query_rows, key_rows, preferred_element_type=jn...  2.09 us
  transfers between devices with their start and end apart: 2, of which 2 were waited for; matrix products, arithmetic and copies ran while one was open for 21% of the time, Pallas kernels for 0%

commit v1 on v0

v1 whole, which is shorter than its diff:
```python
import functools
import math

import jax
import jax.numpy as jnp
from jax import lax
from jax.experimental import pallas as pl
from jax.experimental.pallas import tpu as pltpu
from jax.sharding import PartitionSpec as P

group_blocks = 4
column_chunk = 256
far_below = -1e30
far_above = 1e30
MESH = pl.DeviceIdType.MESH


def other(me, mask, n):
    out = 0
    bit = 1
    while bit < n:
        out = out + lax.rem(lax.div(me, bit) + (mask // bit if isinstance(mask, int) else lax.div(mask, bit)), 2) * bit
        bit *= 2
    return out


def kernel(
    n, hit_ref, prefix_ref, owner_ref, q_ref, new_ref, pool_ref, att_ref, store_ref,
    outgoing, fetched, gathered, chosen, rows, acc, top, total,
    send_sem, recv_sem, new_send, new_recv, pick_send, pick_recv,
):
    slots, heads, block, width = pool_ref.shape
    hd = width // 2
    requests, longest = hit_ref.shape
    groups = q_ref.shape[2] // hd
    columns = groups * block
    scale = math.log2(math.e) / math.sqrt(hd)
    me = lax.axis_index("pool")
    request, head = lax.div(me, heads), lax.rem(me, heads)

    barrier = pltpu.get_barrier_semaphore()
    for d in range(1, n):
        pl.semaphore_signal(barrier, inc=1, device_id={"pool": other(me, d, n)}, device_id_type=MESH)

    def first_owner(r):
        return lax.div(hit_ref[r, 0], slots)

    def stage(target):
        r, g = lax.div(target, heads), lax.rem(target, heads)
        place = lax.rem(me - first_owner(r) + n, n)
        slot = lax.rem(hit_ref[r, jnp.minimum(place, longest - 1)], slots)
        return pool_ref[slot, g]

    def block_copy(d):
        target = other(me, d, n)
        return pltpu.make_async_remote_copy(
            src_ref=outgoing.at[target], dst_ref=fetched.at[me],
            send_sem=send_sem.at[target], recv_sem=recv_sem.at[me],
            device_id={"pool": target}, device_id_type=MESH,
        )

    def block_arrival(source):
        return pltpu.make_async_remote_copy(
            src_ref=outgoing.at[source], dst_ref=fetched.at[source],
            send_sem=send_sem.at[source], recv_sem=recv_sem.at[source],
            device_id={"pool": source}, device_id_type=MESH,
        )

    def new_copy(i):
        target = other(me, i * heads, n)
        return pltpu.make_async_remote_copy(
            src_ref=new_ref.at[0], dst_ref=gathered.at[request],
            send_sem=new_send.at[i], recv_sem=new_recv.at[request],
            device_id={"pool": target}, device_id_type=MESH,
        )

    def new_arrival(i):
        target = other(me, i * heads, n)
        r = lax.div(target, heads)
        return pltpu.make_async_remote_copy(
            src_ref=new_ref.at[0], dst_ref=gathered.at[r],
            send_sem=new_send.at[i], recv_sem=new_recv.at[r],
            device_id={"pool": target}, device_id_type=MESH,
        )

    def pick_copy(i, place):
        target = other(me, i, n)
        return pltpu.make_async_remote_copy(
            src_ref=chosen.at[i], dst_ref=store_ref.at[0, place],
            send_sem=pick_send.at[i], recv_sem=pick_recv.at[place],
            device_id={"pool": target}, device_id_type=MESH,
        )

    def pick(target):
        source, owned = 0, 0
        for r in range(requests):
            here = jnp.where((owner_ref[r, 0] == target) | (owner_ref[r, 1] == target), 1, 0)
            source = source + r * here
            owned = owned + here
        value = gathered[source]
        return jnp.where(owned > 0, value, jnp.zeros_like(value))

    order = []
    for i in range(n // 2):
        order += [n // 2 + i] + ([i + 1] if i + 1 < n // 2 else [])
    for d in order:
        target = other(me, d, n)
        outgoing[target] = stage(target)
    fetched[me] = stage(me)
    gathered[request] = new_ref[0]
    for h in range(groups):
        rows[h * block:(h + 1) * block, :] = q_ref[0, :, h * hd:(h + 1) * hd]
    pl.semaphore_wait(barrier, n - 1)

    for i in range(1, requests):
        new_copy(i).start()
    for d in order:
        block_copy(d).start()

    own_keys, own_values = new_ref[0, :, :hd], new_ref[0, :, hd:].T
    for c in range(0, columns, column_chunk):
        span = slice(c, c + column_chunk)
        s = lax.dot_general(
            own_keys, rows[span, :], (((1,), (1,)), ((), ())), preferred_element_type=jnp.float32
        ) * scale
        key_at = lax.broadcasted_iota(jnp.int32, s.shape, 0)
        token_at = lax.rem(lax.broadcasted_iota(jnp.int32, s.shape, 1), block)
        s = jnp.where(key_at <= token_at, s, far_below)
        m = jnp.max(s, axis=0, keepdims=True)
        w = jnp.where(key_at <= token_at, jnp.exp2(s - m), 0.0)
        top[:, span] = m
        total[:, span] = jnp.sum(w, axis=0, keepdims=True)
        acc[:, span] = jnp.dot(own_values, w.astype(jnp.bfloat16), preferred_element_type=jnp.float32)

    begin = first_owner(request)
    length = prefix_ref[0, request]

    def fold(base):
        stored = fetched.at[pl.ds(base, group_blocks)]
        keys = stored[:, :, :hd].reshape(group_blocks * block, hd)
        values = stored[:, :, hd:].reshape(group_blocks * block, hd).T
        live = [lax.rem(base + j - begin + n, n) < length for j in range(group_blocks)]
        for c in range(0, columns, column_chunk):
            span = slice(c, c + column_chunk)
            s = lax.dot_general(
                keys, rows[span, :], (((1,), (1,)), ((), ())), preferred_element_type=jnp.float32
            ) * scale
            before = top[:, span]
            m = before
            for j in range(group_blocks):
                peak = jnp.max(s[j * block:(j + 1) * block], axis=0, keepdims=True)
                m = jnp.maximum(m, jnp.where(live[j], peak, far_below))
            factor = jnp.exp2(before - m)
            parts = [
                jnp.exp2(s[j * block:(j + 1) * block] - jnp.where(live[j], m, far_above))
                for j in range(group_blocks)
            ]
            w = jnp.concatenate(parts, axis=0)
            top[:, span] = m
            total[:, span] = total[:, span] * factor + jnp.sum(w, axis=0, keepdims=True)
            acc[:, span] = acc[:, span] * factor + jnp.dot(
                values, w.astype(jnp.bfloat16), preferred_element_type=jnp.float32
            )

    for i in range(1, requests):
        new_arrival(i).wait_recv()
    for i in range(1, heads):
        chosen[i] = pick(other(me, i, n))
        pick_copy(i, head).start()
    store_ref[0, head] = pick(me)

    for d in range(1, group_blocks):
        block_arrival(other(me, d, n)).wait_recv()
    fold(lax.div(me, group_blocks) * group_blocks)

    @pl.loop(1, n // group_blocks)
    def _(i):
        base = other(lax.div(me, group_blocks), i, n // group_blocks) * group_blocks
        for j in range(group_blocks):
            block_arrival(base + j).wait_recv()
        fold(base)

    for h in range(groups):
        span = slice(h * block, (h + 1) * block)
        att_ref[0, :, h * hd:(h + 1) * hd] = (acc[:, span] / total[:, span]).T.astype(att_ref.dtype)

    for i in range(1, heads):
        pick_copy(i, lax.rem(other(me, i, n), heads)).wait_recv()
    for i in range(1, heads):
        pick_copy(i, head).wait_send()
    for i in range(1, requests):
        new_copy(i).wait_send()
    for d in order:
        block_copy(d).wait_send()


def on_device(n, queries, new_kv, pool_kv, hit_slots, prefix_blocks, new_owners):
    heads, block, width = pool_kv.shape[1:]
    requests = hit_slots.shape[0]
    hd = width // 2
    columns = queries.shape[2] // hd * block
    smem, vmem = pl.BlockSpec(memory_space=pltpu.SMEM), pl.BlockSpec(memory_space=pltpu.VMEM)
    slab = lambda k: pltpu.VMEM((k, block, width), pool_kv.dtype)
    dma = lambda k: pltpu.SemaphoreType.DMA((k,))
    keys = (n + 1) * block
    return pl.pallas_call(
        functools.partial(kernel, n),
        out_shape=(
            jax.ShapeDtypeStruct(queries.shape, queries.dtype),
            jax.ShapeDtypeStruct((1, heads, block, width), pool_kv.dtype),
        ),
        in_specs=[smem] * 3 + [vmem] * 3,
        out_specs=(vmem, vmem),
        scratch_shapes=[
            slab(n), slab(n), slab(requests), slab(heads),
            pltpu.VMEM((columns, hd), jnp.bfloat16),
            pltpu.VMEM((hd, columns), jnp.float32),
            pltpu.VMEM((1, columns), jnp.float32),
            pltpu.VMEM((1, columns), jnp.float32),
            dma(n), dma(n), dma(requests), dma(requests), dma(heads), dma(heads),
        ],
        compiler_params=pltpu.CompilerParams(
            collective_id=0, has_side_effects=True, vmem_limit_bytes=48 * 2**20
        ),
        cost_estimate=pl.CostEstimate(
            flops=4 * columns * keys * hd,
            bytes_accessed=2 * (pool_kv.size + 2 * queries.size + 2 * heads * block * width),
            transcendentals=columns * keys,
        ),
    )(hit_slots, prefix_blocks[None], new_owners, queries, new_kv, pool_kv)


def solution(mesh):
    placed = (
        P(("grp", "pool"), None, None),
        P(("grp", "pool"), None, None),
        P(("grp", "pool"), None, None, None),
        P("grp", None),
        P("grp"),
        P("grp", None),
    )
    return jax.shard_map(
        functools.partial(on_device, mesh.shape["pool"]),
        mesh=mesh,
        in_specs=placed,
        out_specs=(P(("grp", "pool"), None, None), P(("grp", "pool"), None, None, None)),
        check_vma=False,
    )
```

time: 75.4 us -> 42.6 us (0.56)
  the two profiles are of different devices: /device:TPU:0 before, /device:TPU:13 now
where the time goes in v1:
time: 42.6 us; the launch traced here: 42.3 us
  Pallas kernels  35.8 us (84%)
  local copies, waits for them, and re-layouts  5.87 us (14%)
  between operations  0.66 us (2%)
    pallas_call x1, Pallas kernels, on_device(): pl.pallas_call(functools.partial(kernel, n), out_shape=(jax.ShapeDtypeStr...  35.8 us
    unnamed x14, local copies, waits for them, and re-layouts  5.87 us

profile of v1, /device:TPU:13, one launch (start us, length us, event | category | flops | bytes accessed | tf_op | source)
XLA Modules:
  0.0 42.3 jit_solution(9916235486051908323)
XLA Ops:
  0.6 0.0 copy-start.5
  0.6 0.0 copy-start.3
  0.7 0.6 %copy-done.5 = s32[2]{0:T(128)S(1)} copy-done((s32[2]{0:T(128)S(1)}, s32[2]{0:T(128)}, u32[]{:S(2)}) %copy-start.5) | copy-done | bytes 32
  1.3 0.0 copy-done.3
  1.3 0.0 copy-start
  1.3 1.2 %copy-done = bf16[2,8,128,256]{3,2,1,0:T(8,128)(2,1)S(1)} copy-done((bf16[2,8,128,256]{3,2,1,0:T(8,128)(2,1)S(1)}, bf16[2,8,128,256]{3,2,1,0:T(8,128)(2,1)}, u32[]{:S(2)}) %copy-start) | copy-done | bytes 1048600
  2.6 0.0 copy-start.1
  2.6 0.9 %copy-done.1 = bf16[1,128,1024]{2,1,0:T(8,128)(2,1)S(1)} copy-done((bf16[1,128,1024]{2,1,0:T(8,128)(2,1)S(1)}, bf16[1,128,1024]{2,1,0:T(8,128)(2,1)}, u32[]{:S(2)}) %copy-start.1) | copy-done | bytes 262168
  3.5 0.0 copy-start.2
  3.5 0.8 %copy-done.2 = bf16[1,128,256]{2,1,0:T(8,128)(2,1)S(1)} copy-done((bf16[1,128,256]{2,1,0:T(8,128)(2,1)S(1)}, bf16[1,128,256]{2,1,0:T(8,128)(2,1)}, u32[]{:S(2)}) %copy-start.2) | copy-done | bytes 65560
  4.3 0.0 copy-start.4
  4.3 0.7 %copy-done.4 = s32[2,2]{1,0:T(2,128)S(1)} copy-done((s32[2,2]{1,0:T(2,128)S(1)}, s32[2,2]{1,0:T(2,128)}, u32[]{:S(2)}) %copy-start.4) | copy-done | bytes 40
  5.0 35.8 %shard_map.77 = (bf16[1,128,1024]{2,1,0:T(8,128)(2,1)S(1)}, bf16[1,8,128,256]{3,2,1,0:T(8,128)(2,1)S(1)}) custom-call(s32[2,16]{1,0:T(2,128)S(1)} %copy-done.3, s32[1,2]{1,0:T(1,128)S(1)} %bitcast.1, s32[2,2]{1,0:T(2,128)S(1)} %copy-done.4, bf16[1,128,1024]{2,1,0:T(8,128)(2,1)S(1)} %copy-done.1, bf16[1,128,256]{2,1,0:T(8,128)(2,1)S(1)} %copy-done.2, ...), custom_call_target="tpu_custom_call" | custom-call | flops 1140850688 | bytes 2621440 | tf_op jit(solution)/shard_map/pallas_call | solution.py:206
  40.8 0.7 %copy.10 = bf16[1,128,1024]{2,1,0:T(8,128)(2,1)} copy(bf16[1,128,1024]{2,1,0:T(8,128)(2,1)S(1)} %get-tuple-element.4) | data formatting | bytes 524288
  41.5 0.8 %copy.11 = bf16[1,8,128,256]{3,2,1,0:T(8,128)(2,1)} copy(bf16[1,8,128,256]{3,2,1,0:T(8,128)(2,1)S(1)} %get-tuple-element.5) | data formatting | bytes 1048576
Async XLA Ops:
  0.6 0.7 %copy-start.5 = (s32[2]{0:T(128)S(1)}, s32[2]{0:T(128)}, u32[]{:S(2)}) copy-start(s32[2]{0:T(128)} %param.10) | copy-start | bytes 28
  0.6 0.7 %copy-start.3 = (s32[2,16]{1,0:T(2,128)S(1)}, s32[2,16]{1,0:T(2,128)}, u32[]{:S(2)}) copy-start(s32[2,16]{1,0:T(2,128)} %hit_ref.1) | copy-start | bytes 388
  1.3 1.2 %copy-start = (bf16[2,8,128,256]{3,2,1,0:T(8,128)(2,1)S(1)}, bf16[2,8,128,256]{3,2,1,0:T(8,128)(2,1)}, u32[]{:S(2)}) copy-start(bf16[2,8,128,256]{3,2,1,0:T(8,128)(2,1)} %pool_ref.1) | copy-start | bytes 3145732
  2.6 0.9 %copy-start.1 = (bf16[1,128,1024]{2,1,0:T(8,128)(2,1)S(1)}, bf16[1,128,1024]{2,1,0:T(8,128)(2,1)}, u32[]{:S(2)}) copy-start(bf16[1,128,1024]{2,1,0:T(8,128)(2,1)} %q_ref.1) | copy-start | bytes 786436
  3.5 0.8 %copy-start.2 = (bf16[1,128,256]{2,1,0:T(8,128)(2,1)S(1)}, bf16[1,128,256]{2,1,0:T(8,128)(2,1)}, u32[]{:S(2)}) copy-start(bf16[1,128,256]{2,1,0:T(8,128)(2,1)} %new_ref.1) | copy-start | bytes 196612
  4.3 0.7 %copy-start.4 = (s32[2,2]{1,0:T(2,128)S(1)}, s32[2,2]{1,0:T(2,128)}, u32[]{:S(2)}) copy-start(s32[2,2]{1,0:T(2,128)} %owner_ref.1) | copy-start | bytes 52

commit v2 on v1

--- a/solution.py
+++ b/solution.py
@@ -25,8 +25,8 @@
 
 
 def kernel(
-    n, hit_ref, prefix_ref, owner_ref, q_ref, new_ref, pool_ref, att_ref, store_ref,
-    outgoing, fetched, gathered, chosen, rows, acc, top, total,
+    n, hit_hbm, prefix_hbm, owner_hbm, q_hbm, new_hbm, pool_hbm, att_ref, store_ref,
+    hit_ref, prefix_ref, owner_ref, q_ref, new_ref, pool_ref, in_sem, outgoing, fetched, gathered, chosen, rows, acc, top, total,
     send_sem, recv_sem, new_send, new_recv, pick_send, pick_recv,
 ):
     slots, heads, block, width = pool_ref.shape
@@ -38,6 +38,17 @@
     me = lax.axis_index("pool")
     request, head = lax.div(me, heads), lax.rem(me, heads)
 
+    loads = [
+        pltpu.make_async_copy(hit_hbm, hit_ref, in_sem.at[0]),
+        pltpu.make_async_copy(prefix_hbm, prefix_ref, in_sem.at[1]),
+        pltpu.make_async_copy(owner_hbm, owner_ref, in_sem.at[2]),
+        pltpu.make_async_copy(new_hbm, new_ref, in_sem.at[3]),
+        pltpu.make_async_copy(q_hbm, q_ref, in_sem.at[4]),
+    ] + [
+        pltpu.make_async_copy(pool_hbm.at[k], pool_ref.at[k], in_sem.at[5 + k]) for k in range(slots)
+    ]
+    for load in loads:
+        load.start()
     barrier = pltpu.get_barrier_semaphore()
     for d in range(1, n):
         pl.semaphore_signal(barrier, inc=1, device_id={"pool": other(me, d, n)}, device_id_type=MESH)
@@ -100,6 +111,8 @@
         value = gathered[source]
         return jnp.where(owned > 0, value, jnp.zeros_like(value))
 
+    for load in loads:
+        load.wait()
     order = []
     for i in range(n // 2):
         order += [n // 2 + i] + ([i + 1] if i + 1 < n // 2 else [])
@@ -199,7 +212,7 @@
     requests = hit_slots.shape[0]
     hd = width // 2
     columns = queries.shape[2] // hd * block
-    smem, vmem = pl.BlockSpec(memory_space=pltpu.SMEM), pl.BlockSpec(memory_space=pltpu.VMEM)
+    hbm, vmem = pl.BlockSpec(memory_space=pltpu.HBM), pl.BlockSpec(memory_space=pltpu.VMEM)
     slab = lambda k: pltpu.VMEM((k, block, width), pool_kv.dtype)
     dma = lambda k: pltpu.SemaphoreType.DMA((k,))
     keys = (n + 1) * block
@@ -209,9 +222,13 @@
             jax.ShapeDtypeStruct(queries.shape, queries.dtype),
             jax.ShapeDtypeStruct((1, heads, block, width), pool_kv.dtype),
         ),
-        in_specs=[smem] * 3 + [vmem] * 3,
+        in_specs=[hbm] * 6,
         out_specs=(vmem, vmem),
         scratch_shapes=[
+            pltpu.SMEM(hit_slots.shape, jnp.int32), pltpu.SMEM((1, requests), jnp.int32),
+            pltpu.SMEM(new_owners.shape, jnp.int32),
+            pltpu.VMEM(queries.shape, queries.dtype), pltpu.VMEM(new_kv.shape, new_kv.dtype),
+            pltpu.VMEM(pool_kv.shape, pool_kv.dtype), dma(5 + pool_kv.shape[0]),
             slab(n), slab(n), slab(requests), slab(heads),
             pltpu.VMEM((columns, hd), jnp.bfloat16),
             pltpu.VMEM((hd, columns), jnp.float32),

time: 42.6 us -> 42.2 us (level)
  no operation moved by 1% of the time
where the time goes in v2:
time: 42.2 us; the launch traced here: 41.9 us
  Pallas kernels  35.4 us (84%)
  local copies, waits for them, and re-layouts  5.87 us (14%)
  between operations  0.66 us (2%)
    pallas_call x1, Pallas kernels, on_device(): pl.pallas_call(functools.partial(kernel, n), out_shape=(jax.ShapeDtypeStr...  35.4 us
    unnamed x14, local copies, waits for them, and re-layouts  5.87 us

profile of v2, /device:TPU:13, one launch (start us, length us, event | category | flops | bytes accessed | tf_op | source)
XLA Modules:
  0.0 41.9 jit_solution(8194554560665451325)
XLA Ops:
  0.6 0.0 copy-start.5
  0.6 0.0 copy-start.3
  0.7 0.6 %copy-done.5 = s32[2]{0:T(128)S(1)} copy-done((s32[2]{0:T(128)S(1)}, s32[2]{0:T(128)}, u32[]{:S(2)}) %copy-start.5) | copy-done | bytes 32
  1.3 0.0 copy-done.3
  1.3 0.0 copy-start
  1.3 1.2 %copy-done = bf16[2,8,128,256]{3,2,1,0:T(8,128)(2,1)S(1)} copy-done((bf16[2,8,128,256]{3,2,1,0:T(8,128)(2,1)S(1)}, bf16[2,8,128,256]{3,2,1,0:T(8,128)(2,1)}, u32[]{:S(2)}) %copy-start) | copy-done | bytes 1048600
  2.6 0.0 copy-start.1
  2.6 0.9 %copy-done.1 = bf16[1,128,1024]{2,1,0:T(8,128)(2,1)S(1)} copy-done((bf16[1,128,1024]{2,1,0:T(8,128)(2,1)S(1)}, bf16[1,128,1024]{2,1,0:T(8,128)(2,1)}, u32[]{:S(2)}) %copy-start.1) | copy-done | bytes 262168
  3.5 0.0 copy-start.2
  3.5 0.8 %copy-done.2 = bf16[1,128,256]{2,1,0:T(8,128)(2,1)S(1)} copy-done((bf16[1,128,256]{2,1,0:T(8,128)(2,1)S(1)}, bf16[1,128,256]{2,1,0:T(8,128)(2,1)}, u32[]{:S(2)}) %copy-start.2) | copy-done | bytes 65560
  4.3 0.0 copy-start.4
  4.3 0.7 %copy-done.4 = s32[2,2]{1,0:T(2,128)S(1)} copy-done((s32[2,2]{1,0:T(2,128)S(1)}, s32[2,2]{1,0:T(2,128)}, u32[]{:S(2)}) %copy-start.4) | copy-done | bytes 40
  5.0 35.4 %shard_map.77 = (bf16[1,128,1024]{2,1,0:T(8,128)(2,1)S(1)}, bf16[1,8,128,256]{3,2,1,0:T(8,128)(2,1)S(1)}) custom-call(s32[2,16]{1,0:T(2,128)S(1)} %copy-done.3, s32[1,2]{1,0:T(1,128)S(1)} %bitcast.1, s32[2,2]{1,0:T(2,128)S(1)} %copy-done.4, bf16[1,128,1024]{2,1,0:T(8,128)(2,1)S(1)} %copy-done.1, bf16[1,128,256]{2,1,0:T(8,128)(2,1)S(1)} %copy-done.2, ...), custom_call_target="tpu_custom_call" | custom-call | flops 1140850688 | bytes 2621440 | tf_op jit(solution)/shard_map/pallas_call | solution.py:219
  40.5 0.7 %copy.10 = bf16[1,128,1024]{2,1,0:T(8,128)(2,1)} copy(bf16[1,128,1024]{2,1,0:T(8,128)(2,1)S(1)} %get-tuple-element.4) | data formatting | bytes 524288
  41.2 0.8 %copy.11 = bf16[1,8,128,256]{3,2,1,0:T(8,128)(2,1)} copy(bf16[1,8,128,256]{3,2,1,0:T(8,128)(2,1)S(1)} %get-tuple-element.5) | data formatting | bytes 1048576
Async XLA Ops:
  0.6 0.7 %copy-start.5 = (s32[2]{0:T(128)S(1)}, s32[2]{0:T(128)}, u32[]{:S(2)}) copy-start(s32[2]{0:T(128)} %param.10) | copy-start | bytes 28
  0.6 0.7 %copy-start.3 = (s32[2,16]{1,0:T(2,128)S(1)}, s32[2,16]{1,0:T(2,128)}, u32[]{:S(2)}) copy-start(s32[2,16]{1,0:T(2,128)} %hit_hbm.1) | copy-start | bytes 388
  1.3 1.2 %copy-start = (bf16[2,8,128,256]{3,2,1,0:T(8,128)(2,1)S(1)}, bf16[2,8,128,256]{3,2,1,0:T(8,128)(2,1)}, u32[]{:S(2)}) copy-start(bf16[2,8,128,256]{3,2,1,0:T(8,128)(2,1)} %pool_hbm.1) | copy-start | bytes 3145732
  2.6 0.9 %copy-start.1 = (bf16[1,128,1024]{2,1,0:T(8,128)(2,1)S(1)}, bf16[1,128,1024]{2,1,0:T(8,128)(2,1)}, u32[]{:S(2)}) copy-start(bf16[1,128,1024]{2,1,0:T(8,128)(2,1)} %q_hbm.1) | copy-start | bytes 786436
  3.5 0.8 %copy-start.2 = (bf16[1,128,256]{2,1,0:T(8,128)(2,1)S(1)}, bf16[1,128,256]{2,1,0:T(8,128)(2,1)}, u32[]{:S(2)}) copy-start(bf16[1,128,256]{2,1,0:T(8,128)(2,1)} %new_hbm.1) | copy-start | bytes 196612
  4.3 0.7 %copy-start.4 = (s32[2,2]{1,0:T(2,128)S(1)}, s32[2,2]{1,0:T(2,128)}, u32[]{:S(2)}) copy-start(s32[2,2]{1,0:T(2,128)} %owner_hbm.1) | copy-start | bytes 52

commit v3 on v2

--- a/solution.py
+++ b/solution.py
@@ -237,7 +237,7 @@
             dma(n), dma(n), dma(requests), dma(requests), dma(heads), dma(heads),
         ],
         compiler_params=pltpu.CompilerParams(
-            collective_id=0, has_side_effects=True, vmem_limit_bytes=48 * 2**20
+            collective_id=0, has_side_effects=True, vmem_limit_bytes=56 * 2**20
         ),
         cost_estimate=pl.CostEstimate(
             flops=4 * columns * keys * hd,

time: 42.2 us -> 39.5 us (0.936)
  local copies, waits for them, and re-layouts: 5.87 us -> 2.52 us
  Pallas kernels: 35.4 us -> 36.2 us
    unnamed x14 -> x4, local copies, waits for them, and re-layouts: 5.87 us -> 2.52 us
    pallas_call x1, Pallas kernels: 35.4 us -> 36.2 us  [on_device(): pl.pallas_call(functools.partial(kernel, n), out_shape=(jax.ShapeDtypeStr...]
where the time goes in v3:
time: 39.5 us; the launch traced here: 39.3 us
  Pallas kernels  36.2 us (92%)
  local copies, waits for them, and re-layouts  2.52 us (6%)
  between operations  0.65 us (2%)
    pallas_call x1, Pallas kernels, on_device(): pl.pallas_call(functools.partial(kernel, n), out_shape=(jax.ShapeDtypeStr...  36.2 us
    unnamed x4, local copies, waits for them, and re-layouts  2.52 us

profile of v3, /device:TPU:13, one launch (start us, length us, event | category | flops | bytes accessed | tf_op | source)
XLA Modules:
  0.0 39.3 jit_solution(1326331948867488391)
XLA Ops:
  0.6 36.2 %shard_map.77 = (bf16[1,128,1024]{2,1,0:T(8,128)(2,1)}, bf16[1,8,128,256]{3,2,1,0:T(8,128)(2,1)}) custom-call(s32[2,16]{1,0:T(2,128)} %hit_hbm.1, s32[1,2]{1,0:T(1,128)} %bitcast.1, s32[2,2]{1,0:T(2,128)} %owner_hbm.1, bf16[1,128,1024]{2,1,0:T(8,128)(2,1)} %q_hbm.1, bf16[1,128,256]{2,1,0:T(8,128)(2,1)} %new_hbm.1, bf16[2,8,128,256]{3,2,1,0:T(8,128)(2,1)} %pool_hbm.1), custom_call_target="tpu_custom_call" | custom-call | flops 1140850688 | bytes 2621440 | tf_op jit(solution)/shard_map/pallas_call | solution.py:219
  36.8 0.0 copy-start
  36.8 1.7 %copy.10 = bf16[1,128,1024]{2,1,0:T(8,128)(2,1)} copy(bf16[1,128,1024]{2,1,0:T(8,128)(2,1)} %get-tuple-element.4) | data formatting | bytes 524288
  38.5 0.0 copy-done
  38.5 0.8 %copy.11 = bf16[1,8,128,256]{3,2,1,0:T(8,128)(2,1)} copy(bf16[1,8,128,256]{3,2,1,0:T(8,128)(2,1)S(1)} %copy-done) | data formatting | bytes 1048576
Async XLA Ops:
  36.8 1.7 %copy-start = (bf16[1,8,128,256]{3,2,1,0:T(8,128)(2,1)S(1)}, bf16[1,8,128,256]{3,2,1,0:T(8,128)(2,1)}, u32[]{:S(2)}) copy-start(bf16[1,8,128,256]{3,2,1,0:T(8,128)(2,1)} %get-tuple-element.5) | copy-start | bytes 1572868

commit v4 on v3

--- a/solution.py
+++ b/solution.py
@@ -8,7 +8,7 @@
 from jax.experimental.pallas import tpu as pltpu
 from jax.sharding import PartitionSpec as P
 
-group_blocks = 4
+group_blocks = 2
 column_chunk = 256
 far_below = -1e30
 far_above = 1e30

time: 39.5 us -> 39 us (0.987)
  Pallas kernels: 36.2 us -> 35.7 us
    pallas_call x1, Pallas kernels: 36.2 us -> 35.7 us  [on_device(): pl.pallas_call(functools.partial(kernel, n), out_shape=(jax.ShapeDtypeStr...]
where the time goes in v4:
time: 39 us; the launch traced here: 38.9 us
  Pallas kernels  35.7 us (92%)
  local copies, waits for them, and re-layouts  2.52 us (6%)
  between operations  0.65 us (2%)
    pallas_call x1, Pallas kernels, on_device(): pl.pallas_call(functools.partial(kernel, n), out_shape=(jax.ShapeDtypeStr...  35.7 us
    unnamed x4, local copies, waits for them, and re-layouts  2.52 us

profile of v4, /device:TPU:13, one launch (start us, length us, event | category | flops | bytes accessed | tf_op | source)
XLA Modules:
  0.0 38.9 jit_solution(10792633699863408010)
XLA Ops:
  0.6 35.7 %shard_map.77 = (bf16[1,128,1024]{2,1,0:T(8,128)(2,1)}, bf16[1,8,128,256]{3,2,1,0:T(8,128)(2,1)}) custom-call(s32[2,16]{1,0:T(2,128)} %hit_hbm.1, s32[1,2]{1,0:T(1,128)} %bitcast.1, s32[2,2]{1,0:T(2,128)} %owner_hbm.1, bf16[1,128,1024]{2,1,0:T(8,128)(2,1)} %q_hbm.1, bf16[1,128,256]{2,1,0:T(8,128)(2,1)} %new_hbm.1, bf16[2,8,128,256]{3,2,1,0:T(8,128)(2,1)} %pool_hbm.1), custom_call_target="tpu_custom_call" | custom-call | flops 1140850688 | bytes 2621440 | tf_op jit(solution)/shard_map/pallas_call | solution.py:219
  36.3 0.0 copy-start
  36.3 1.7 %copy.10 = bf16[1,128,1024]{2,1,0:T(8,128)(2,1)} copy(bf16[1,128,1024]{2,1,0:T(8,128)(2,1)} %get-tuple-element.4) | data formatting | bytes 524288
  38.1 0.0 copy-done
  38.1 0.8 %copy.11 = bf16[1,8,128,256]{3,2,1,0:T(8,128)(2,1)} copy(bf16[1,8,128,256]{3,2,1,0:T(8,128)(2,1)S(1)} %copy-done) | data formatting | bytes 1048576
Async XLA Ops:
  36.3 1.7 %copy-start = (bf16[1,8,128,256]{3,2,1,0:T(8,128)(2,1)S(1)}, bf16[1,8,128,256]{3,2,1,0:T(8,128)(2,1)}, u32[]{:S(2)}) copy-start(bf16[1,8,128,256]{3,2,1,0:T(8,128)(2,1)} %get-tuple-element.5) | copy-start | bytes 1572868

commit v5 on v4

--- a/solution.py
+++ b/solution.py
@@ -111,7 +111,7 @@
         value = gathered[source]
         return jnp.where(owned > 0, value, jnp.zeros_like(value))
 
-    for load in loads:
+    for load in loads[:4] + loads[5:]:
         load.wait()
     order = []
     for i in range(n // 2):
@@ -121,14 +121,16 @@
         outgoing[target] = stage(target)
     fetched[me] = stage(me)
     gathered[request] = new_ref[0]
-    for h in range(groups):
-        rows[h * block:(h + 1) * block, :] = q_ref[0, :, h * hd:(h + 1) * hd]
     pl.semaphore_wait(barrier, n - 1)
 
     for i in range(1, requests):
         new_copy(i).start()
     for d in order:
         block_copy(d).start()
+
+    loads[4].wait()
+    for h in range(groups):
+        rows[h * block:(h + 1) * block, :] = q_ref[0, :, h * hd:(h + 1) * hd]
 
     own_keys, own_values = new_ref[0, :, :hd], new_ref[0, :, hd:].T
     for c in range(0, columns, column_chunk):
@@ -207,6 +209,22 @@
         block_copy(d).wait_send()
 
 
+def settle(att_ref, store_ref, att_out, store_out, att_held, store_held, in_sem, out_sem):
+    pieces = []
+    for source, held, target in ((att_ref, att_held, att_out), (store_ref, store_held, store_out)):
+        size = source.shape[1] // 4
+        pieces += [tuple(x.at[0, pl.ds(k * size, size)] for x in (source, held, target)) for k in range(4)]
+    loads = [pltpu.make_async_copy(x, y, in_sem.at[k]) for k, (x, y, _) in enumerate(pieces)]
+    stores = [pltpu.make_async_copy(y, z, out_sem.at[k]) for k, (_, y, z) in enumerate(pieces)]
+    for load in loads:
+        load.start()
+    for load, keep in zip(loads, stores):
+        load.wait()
+        keep.start()
+    for keep in stores:
+        keep.wait()
+
+
 def on_device(n, queries, new_kv, pool_kv, hit_slots, prefix_blocks, new_owners):
     heads, block, width = pool_kv.shape[1:]
     requests = hit_slots.shape[0]
@@ -216,7 +234,7 @@
     slab = lambda k: pltpu.VMEM((k, block, width), pool_kv.dtype)
     dma = lambda k: pltpu.SemaphoreType.DMA((k,))
     keys = (n + 1) * block
-    return pl.pallas_call(
+    att, store = pl.pallas_call(
         functools.partial(kernel, n),
         out_shape=(
             jax.ShapeDtypeStruct(queries.shape, queries.dtype),
@@ -245,6 +263,16 @@
             transcendentals=columns * keys,
         ),
     )(hit_slots, prefix_blocks[None], new_owners, queries, new_kv, pool_kv)
+    anywhere = pl.BlockSpec(memory_space=pl.ANY)
+    return pl.pallas_call(
+        settle,
+        out_shape=tuple(jax.ShapeDtypeStruct(x.shape, x.dtype) for x in (att, store)),
+        in_specs=[anywhere] * 2,
+        out_specs=(hbm, hbm),
+        scratch_shapes=[
+            pltpu.VMEM(att.shape, att.dtype), pltpu.VMEM(store.shape, store.dtype), dma(8), dma(8)
+        ],
+    )(att, store)
 
 
 def solution(mesh):

time: 39 us -> 38.5 us (0.987)
  local copies, waits for them, and re-layouts: 2.52 us -> 0 us
  Pallas kernels: 35.7 us -> 37.7 us
    unnamed x4 -> x0, local copies, waits for them, and re-layouts: 2.52 us -> none
    pallas_call x0 -> x1, Pallas kernels: none -> 2.01 us  [on_device(): pl.pallas_call(settle, out_shape=tuple((jax.ShapeDtypeStruct(x.shape, x.d...]
where the time goes in v5:
time: 38.5 us; the launch traced here: 38.3 us
  Pallas kernels  37.7 us (98%)
  between operations  0.64 us (2%)
    pallas_call x1, Pallas kernels, on_device(): pl.pallas_call(functools.partial(kernel, n), out_shape=(jax.ShapeDtypeStr...  35.7 us
    pallas_call x1, Pallas kernels, on_device(): pl.pallas_call(settle, out_shape=tuple((jax.ShapeDtypeStruct(x.shape, x.d...  2.01 us

profile of v5, /device:TPU:13, one launch (start us, length us, event | category | flops | bytes accessed | tf_op | source)
XLA Modules:
  0.0 38.3 jit_solution(14255761295081433129)
XLA Ops:
  0.6 35.7 %shard_map.77 = (bf16[1,128,1024]{2,1,0:T(8,128)(2,1)}, bf16[1,8,128,256]{3,2,1,0:T(8,128)(2,1)}) custom-call(s32[2,16]{1,0:T(2,128)} %hit_hbm.1, s32[1,2]{1,0:T(1,128)} %bitcast.1, s32[2,2]{1,0:T(2,128)} %owner_hbm.1, bf16[1,128,1024]{2,1,0:T(8,128)(2,1)} %q_hbm.1, bf16[1,128,256]{2,1,0:T(8,128)(2,1)} %new_hbm.1, bf16[2,8,128,256]{3,2,1,0:T(8,128)(2,1)} %pool_hbm.1), custom_call_target="tpu_custom_call" | custom-call | flops 1140850688 | bytes 2621440 | tf_op jit(solution)/shard_map/pallas_call | solution.py:237
  36.3 2.0 %shard_map.78 = (bf16[1,128,1024]{2,1,0:T(8,128)(2,1)}, bf16[1,8,128,256]{3,2,1,0:T(8,128)(2,1)}) custom-call(bf16[1,128,1024]{2,1,0:T(8,128)(2,1)} %get-tuple-element.4.att_ref, bf16[1,8,128,256]{3,2,1,0:T(8,128)(2,1)} %get-tuple-element.5.store_ref), custom_call_target="tpu_custom_call" | custom-call | tf_op jit(solution)/shard_map/pallas_call | solution.py:267

commit v6 on v5

--- a/solution.py
+++ b/solution.py
@@ -9,7 +9,7 @@
 from jax.sharding import PartitionSpec as P
 
 group_blocks = 2
-column_chunk = 256
+column_chunk = 128
 far_below = -1e30
 far_above = 1e30
 MESH = pl.DeviceIdType.MESH

time: 38.5 us -> 38 us (0.987)
  Pallas kernels: 37.7 us -> 37.2 us
    pallas_call x1, Pallas kernels: 35.7 us -> 35.2 us  [on_device(): pl.pallas_call(functools.partial(kernel, n), out_shape=(jax.ShapeDtypeStr...]
where the time goes in v6:
time: 38 us; the launch traced here: 37.9 us
  Pallas kernels  37.2 us (98%)
  between operations  0.64 us (2%)
    pallas_call x1, Pallas kernels, on_device(): pl.pallas_call(functools.partial(kernel, n), out_shape=(jax.ShapeDtypeStr...  35.2 us
    pallas_call x1, Pallas kernels, on_device(): pl.pallas_call(settle, out_shape=tuple((jax.ShapeDtypeStruct(x.shape, x.d...  2.01 us

profile of v6, /device:TPU:13, one launch (start us, length us, event | category | flops | bytes accessed | tf_op | source)
XLA Modules:
  0.0 37.9 jit_solution(10528730783123676545)
XLA Ops:
  0.6 35.2 %shard_map.77 = (bf16[1,128,1024]{2,1,0:T(8,128)(2,1)}, bf16[1,8,128,256]{3,2,1,0:T(8,128)(2,1)}) custom-call(s32[2,16]{1,0:T(2,128)} %hit_hbm.1, s32[1,2]{1,0:T(1,128)} %bitcast.1, s32[2,2]{1,0:T(2,128)} %owner_hbm.1, bf16[1,128,1024]{2,1,0:T(8,128)(2,1)} %q_hbm.1, bf16[1,128,256]{2,1,0:T(8,128)(2,1)} %new_hbm.1, bf16[2,8,128,256]{3,2,1,0:T(8,128)(2,1)} %pool_hbm.1), custom_call_target="tpu_custom_call" | custom-call | flops 1140850688 | bytes 2621440 | tf_op jit(solution)/shard_map/pallas_call | solution.py:237
  35.8 2.0 %shard_map.78 = (bf16[1,128,1024]{2,1,0:T(8,128)(2,1)}, bf16[1,8,128,256]{3,2,1,0:T(8,128)(2,1)}) custom-call(bf16[1,128,1024]{2,1,0:T(8,128)(2,1)} %get-tuple-element.4.att_ref, bf16[1,8,128,256]{3,2,1,0:T(8,128)(2,1)} %get-tuple-element.5.store_ref), custom_call_target="tpu_custom_call" | custom-call | tf_op jit(solution)/shard_map/pallas_call | solution.py:267
